TPU v7x, 32 devices: a whole 2x2x4 slice. The times are simulated.
32 devices in a mesh: fsdp: 16 (over z, y, x), replica: 2 (over core).
Axes of the slice: x: 2, y: 2, z: 4, core: 2. Of those that a mesh axis runs over, the one named last changes fastest.
Arguments:
- master: float32 [1024, 8192], P('fsdp', 'replica'), may hold values from -6 to 6
- moment_one: float32 [1024, 8192], P('fsdp', 'replica'), may hold values from -6 to 6
- moment_two: float32 [1024, 8192], P('fsdp', 'replica'), may hold values from 0.5 to 8
- gradients: float32 [2, 1024, 8192], P('replica', 'fsdp'), may hold values from -6 to 6
- new_row: int32 [1024], P('fsdp'), may hold values from 0 to 1023, as said below
Outputs:
- new_master: float32 [1024, 8192], P('fsdp', 'replica')
- new_moment_one: float32 [1024, 8192], P('fsdp', 'replica')
- new_moment_two: float32 [1024, 8192], P('fsdp', 'replica')
- params: bfloat16 [1024, 8192], P('fsdp')
- checksum: float32 [1024], P('fsdp')
Inputs may be any that keep to these rules, and one draw needn't show every extreme that they name: new_row is a permutation; the 64 old rows of one fsdp index send at most 8 rows to the 64 new rows of any one fsdp index, and this most is reached.
All inputs are finite; a program needn't handle non-finite values.
Results may differ from a plain program's by a relative error of at most 0.0025.
Values may be sent and summed in bfloat16 or wider, within the bound.
No kernel may reach another device: no remote copies, remote signals or barrier semaphores. Data moves between devices by JAX's collectives and lax.ppermute only.
A program may use at most 128 MiB of HBM per device.

v0:
```python
import math

import jax
import jax.numpy as jnp
from jax import lax
from jax.sharding import PartitionSpec as P


def placement_order(got_offset, rows_dev):
    flat = got_offset.reshape(-1)
    index = jnp.arange(flat.shape[0], dtype=jnp.int32)
    wanted = jnp.arange(rows_dev, dtype=jnp.int32)
    hits = (flat[None, :] == wanted[:, None]).astype(jnp.int32)
    return jnp.sum(hits * index[None, :], axis=1)


def shards(master, moment_one, moment_two, gradients, new_row):
    rows_dev, width = master.shape
    peers = lax.axis_size("fsdp")
    copies = lax.axis_size("replica")
    capacity = max(2, 2 * rows_dev // peers)
    target = new_row // rows_dev
    offset = new_row % rows_dev
    local = jnp.arange(rows_dev, dtype=jnp.int32)
    earlier = (target[:, None] == target[None, :]) & (local[None, :] < local[:, None])
    rank = jnp.sum(earlier.astype(jnp.int32), axis=1)
    owners = jnp.arange(peers, dtype=jnp.int32)
    slots = jnp.arange(capacity, dtype=jnp.int32)
    match = (
        (target[None, None, :] == owners[:, None, None])
        & (rank[None, None, :] == slots[None, :, None])
    ).astype(jnp.int32)
    source_row = jnp.sum(match * local[None, None, :], axis=2).reshape(-1)
    filled = jnp.sum(match, axis=2)
    send_offset = jnp.where(filled > 0, jnp.sum(match * offset[None, None, :], axis=2), -1)
    states = jnp.stack([master, moment_one, moment_two], axis=1)
    send_states = jnp.take(states, source_row, axis=0).reshape(peers, capacity, 3, width)
    send_grads = jnp.take(gradients[0], source_row, axis=0).reshape(peers, capacity, width * copies)
    got_states, got_grads, got_offset = (
        lax.all_to_all(send_states, "fsdp", split_axis=0, concat_axis=0, tiled=True),
        lax.all_to_all(send_grads, "fsdp", split_axis=0, concat_axis=0, tiled=True),
        lax.all_to_all(send_offset, "fsdp", split_axis=0, concat_axis=0, tiled=True),
    )
    order = placement_order(got_offset, rows_dev)
    moved = jnp.take(got_states.reshape(peers * capacity, 3, width), order, axis=0)
    full_grads = jnp.take(got_grads.reshape(peers * capacity, width * copies), order, axis=0)
    summed = lax.psum_scatter(
        full_grads.astype(jnp.bfloat16), "replica", scatter_dimension=1, tiled=True
    ).astype(jnp.float32)
    moved_master = moved[:, 0]
    moved_one = moved[:, 1]
    moved_two = moved[:, 2]
    column = lax.axis_index("replica") * width + jnp.arange(width, dtype=jnp.int32)
    weights = 1.0 + (column % 7).astype(jnp.float32) / 7.0
    partial_sum = jnp.sum(moved_master * weights[None, :], axis=1) / math.sqrt(width * copies)
    checksum = lax.psum(partial_sum, "replica")
    new_one = 0.9 * moved_one + 0.1 * summed
    new_two = 0.95 * moved_two + 0.05 * summed * summed
    update = new_one / (1.0 - 0.9**10) / (jnp.sqrt(new_two / (1.0 - 0.95**10)) + 1e-08)
    new_master = moved_master - 0.05 * (update + 0.1 * moved_master)
    params = lax.all_gather(new_master.astype(jnp.bfloat16), "replica", axis=1, tiled=True)
    return (new_master, new_one, new_two, params, checksum)


def solution(mesh):
    return jax.shard_map(
        shards,
        mesh=mesh,
        in_specs=(
            P("fsdp", "replica"),
            P("fsdp", "replica"),
            P("fsdp", "replica"),
            P("replica", "fsdp", None),
            P("fsdp"),
        ),
        out_specs=(
            P("fsdp", "replica"),
            P("fsdp", "replica"),
            P("fsdp", "replica"),
            P("fsdp", None),
            P("fsdp"),
        ),
        check_vma=False,
    )
```

profile of v0, /device:TPU:5, one launch (start us, length us, event | category | flops | bytes accessed | tf_op | source)
XLA Modules:
  0.0 274.4 jit_solution(8426438716788204983)
XLA Ops:
  8.2 0.9 fusion.3
  9.7 6.7 %all-to-all-start = ((s32[16,1,8]{2,1,0:T(1,128)}), s32[16,1,8]{2,1,0:T(1,128)S(1)}, u32[]{:S(2)}, u32[]{:S(2)}) async-start(s32[16,1,8]{2,1,0:T(1,128)} %bitcast.11), calls=%async_computation | async-start | bytes 16384 | tf_op jit(solution)/shard_map/all_to_all | solution.py:42
  16.6 3.3 %gather_fusion.2 = bf16[128,8192]{1,0:T(8,128)(2,1)} fusion(f32[64,8192]{1,0:T(8,128)S(1)} %bitcast.30, s32[1024]{0:T(1024)S(1)} %pad_clamp_fusion.1), kind=kCustom, calls=%fused_computation.2 | custom fusion | bytes 4194816 | tf_op jit(solution)/shard_map/jit(_take)/gather | solution.py:38
  19.9 3.5 %bitcast_select_fusion = bf16[16,8,8192]{2,1,0:T(8,128)(2,1)} fusion(bf16[128,8192]{1,0:T(8,128)(2,1)} %gather_fusion.2, pred[16,8]{1,0:T(8,128)(4,1)S(1)} %compare_and_fusion), kind=kLoop, calls=%fused_computation.6 | loop fusion | flops 1048576 | bytes 4194432 | tf_op jit(solution)/shard_map/jit(_take)/select_n | solution.py:38
  23.3 6.4 %all-to-all-start.2 = ((bf16[16,8,8192]{2,1,0:T(8,128)(2,1)}), bf16[16,8,8192]{2,1,0:T(8,128)(2,1)S(1)}, u32[]{:S(2)}, u32[]{:S(2)}) async-start(bf16[16,8,8192]{2,1,0:T(8,128)(2,1)} %bitcast_select_fusion), calls=%async_computation.2 | async-start | bytes 4194304 | tf_op jit(solution)/shard_map/all_to_all | solution.py:41
  29.7 1.2 stack.12
  30.9 2.4 stack.13
  33.3 1.2 stack.14
  34.5 4.5 %pad_maximum_fusion = f32[64,3,4096]{2,1,0:T(4,128)} fusion(f32[64,1,4096]{2,1,0:T(1,128)S(1)} %stack.14, f32[64,1,4096]{2,1,0:T(1,128)S(1)} %stack.13, f32[64,1,4096]{2,1,0:T(1,128)S(1)} %stack.12), kind=kLoop, calls=%fused_computation.5 | loop fusion | flops 1572864 | bytes 6291456 | tf_op jit(solution)/shard_map/stack | solution.py:36
  39.0 11.5 %gather_fusion = f32[128,3,4096]{2,1,0:T(4,128)} fusion(f32[64,3,4096]{2,1,0:T(4,128)} %pad_maximum_fusion, s32[1024]{0:T(1024)S(1)} %pad_clamp_fusion.1), kind=kCustom, calls=%fused_computation | custom fusion | bytes 12583424 | tf_op jit(solution)/shard_map/jit(_take)/gather | solution.py:37
  50.5 11.6 %copy_select_fusion = f32[16,8,3,4096]{3,1,2,0:T(8,128)} fusion(f32[16,8,3,4096]{3,2,1,0:T(4,128)} %bitcast.32, pred[16,8]{1,0:T(8,128)(4,1)S(1)} %compare_and_fusion), kind=kLoop, calls=%fused_computation.4 | loop fusion | flops 1572864 | bytes 12583040 | tf_op jit(solution)/shard_map/jit(_take)/select_n | solution.py:37
  62.1 11.0 %all-to-all-done.2 = bf16[16,8,8192]{2,1,0:T(8,128)(2,1)S(1)} async-done(((bf16[16,8,8192]{2,1,0:T(8,128)(2,1)}), bf16[16,8,8192]{2,1,0:T(8,128)(2,1)S(1)}, u32[]{:S(2)}, u32[]{:S(2)}) %all-to-all-start.2) | async-done | bytes 2097184 | tf_op jit(solution)/shard_map/all_to_all | solution.py:41
  73.1 8.8 %all-to-all-start.1 = ((f32[16,8,3,4096]{3,1,2,0:T(8,128)}), f32[16,8,3,4096]{3,1,2,0:T(8,128)}, u32[]{:S(2)}, u32[]{:S(2)}) async-start(f32[16,8,3,4096]{3,1,2,0:T(8,128)} %copy_select_fusion), calls=%async_computation.1 | async-start | bytes 12582912 | tf_op jit(solution)/shard_map/all_to_all | solution.py:40
  83.5 1.2 gather_fusion.3
  84.7 1.2 select_convert_fusion
  86.2 119.5 %all-to-all-done.1 = f32[16,8,3,4096]{3,1,2,0:T(8,128)} async-done(((f32[16,8,3,4096]{3,1,2,0:T(8,128)}), f32[16,8,3,4096]{3,1,2,0:T(8,128)}, u32[]{:S(2)}, u32[]{:S(2)}) %all-to-all-start.1) | async-done | bytes 6291488 | tf_op jit(solution)/shard_map/all_to_all | solution.py:40
  205.7 10.4 %copy.31 = f32[16,8,3,4096]{3,2,1,0:T(4,128)} copy(f32[16,8,3,4096]{3,1,2,0:T(8,128)} %all-to-all-done.1) | data formatting | bytes 12582912 | tf_op jit(solution)/shard_map/all_to_all | solution.py:40
  216.1 8.1 %gather_fusion.1 = f32[64,3,4096]{2,1,0:T(4,128)} fusion(f32[128,3,4096]{2,1,0:T(4,128)} %bitcast.33, s32[1024]{0:T(1024)S(1)} %pad_clamp_fusion), kind=kCustom, calls=%fused_computation.1 | custom fusion | bytes 6291712 | tf_op jit(solution)/shard_map/jit(_take)/gather | solution.py:45
  224.3 3.3 %broadcast_select_fusion = f32[64,3,4096]{2,1,0:T(4,128)S(1)} fusion(f32[64,3,4096]{2,1,0:T(4,128)} %gather_fusion.1, pred[64]{0:T(512)(128)(4,1)S(1)} %compare_and_fusion.1), kind=kLoop, calls=%fused_computation.8 | loop fusion | flops 786432 | bytes 6291520 | tf_op jit(solution)/shard_map/jit(_take)/select_n | solution.py:45
  227.6 4.8 %slice_multiply_fusion = (f32[64,1,4096]{2,1,0:T(1,128)S(1)}, f32[64,1,4096]{2,1,0:T(1,128)}, f32[64,1,4096]{2,1,0:T(1,128)}) fusion(f32[64,3,4096]{2,1,0:T(4,128)S(1)} %broadcast_select_fusion), kind=kLoop, calls=%fused_computation.13 | loop fusion | flops 262144 | bytes 6291456 | tf_op jit(solution)/shard_map/mul | solution.py:58
  232.4 6.5 %fusion.15 = (bf16[64,4096]{1,0:T(8,128)(2,1)}, f32[64,4096]{1,0:T(8,128)}, f32[64,4096]{1,0:T(8,128)}, f32[64,4096]{1,0:T(8,128)}, f32[64]{0:T(128)S(1)}) fusion(f32[64,1,4096]{2,1,0:T(1,128)} %get-tuple-element.13, bf16[64,4096]{1,0:T(8,128)(2,1)} %reduce-scatter.2.cloned.1.call-done, f32[64,1,4096]{2,1,0:T(1,128)} %get-tuple-element.14, ...), kind=kLoop, calls=%fused_computation.57 | loop fusion | flops 4718528 | bytes 7356672 | tf_op jit(solution)/shard_map/convert_element_type | solution.py:61
  238.9 5.2 %psum.7 = f32[64]{0:T(128)} all-reduce(f32[64]{0:T(128)S(1)} %broadcast_multiply_fusion), channel_id=1, replica_groups=mesh['fsdp'=16,'replica'=2] {'replica'}, use_global_device_ids=true, to_apply=%region_7.8 | all-reduce | flops 64 | bytes 512 | tf_op jit(solution)/shard_map/psum | solution.py:56
  244.1 21.2 %all-gather.2.cloned.1.call-done = bf16[64,8192]{1,0:T(8,128)(2,1)} async-done(((bf16[64,4096]{1,0:T(8,128)(2,1)}), bf16[64,8192]{1,0:T(8,128)(2,1)}) %all-gather.2.cloned.1.call-update) | async-done | bytes 1048592 | tf_op jit(solution)/shard_map/all_gather | solution.py:61
  265.3 2.3 copy.55
  (32 shorter events, 3.5 us)
Async XLA Ops:
  7.2 9.4 %copy-start = (f32[1,64,8192]{2,1,0:T(8,128)S(1)}, f32[1,64,8192]{2,1,0:T(8,128)}, u32[]{:S(2)}) copy-start(f32[1,64,8192]{2,1,0:T(8,128)} %param.8) | copy-start | bytes 6291460
  9.7 13.6 %all-to-all-start = ((s32[16,1,8]{2,1,0:T(1,128)}), s32[16,1,8]{2,1,0:T(1,128)S(1)}, u32[]{:S(2)}, u32[]{:S(2)}) async-start(s32[16,1,8]{2,1,0:T(1,128)} %bitcast.11), calls=%async_computation | async-start | bytes 16384 | tf_op jit(solution)/shard_map/all_to_all | solution.py:42
  19.9 9.8 %copy-start.2 = (f32[64,4096]{1,0:T(8,128)S(1)}, f32[64,4096]{1,0:T(8,128)}, u32[]{:S(2)}) copy-start(f32[64,4096]{1,0:T(8,128)} %param.5) | copy-start | bytes 3145732
  23.3 49.8 %all-to-all-start.2 = ((bf16[16,8,8192]{2,1,0:T(8,128)(2,1)}), bf16[16,8,8192]{2,1,0:T(8,128)(2,1)S(1)}, u32[]{:S(2)}, u32[]{:S(2)}) async-start(bf16[16,8,8192]{2,1,0:T(8,128)(2,1)} %bitcast_select_fusion), calls=%async_computation.2 | async-start | bytes 4194304 | tf_op jit(solution)/shard_map/all_to_all | solution.py:41
  29.7 3.6 %copy-start.3 = (f32[64,4096]{1,0:T(8,128)S(1)}, f32[64,4096]{1,0:T(8,128)}, u32[]{:S(2)}) copy-start(f32[64,4096]{1,0:T(8,128)} %param.7) | copy-start | bytes 3145732
  73.1 132.6 %all-to-all-start.1 = ((f32[16,8,3,4096]{3,1,2,0:T(8,128)}), f32[16,8,3,4096]{3,1,2,0:T(8,128)}, u32[]{:S(2)}, u32[]{:S(2)}) async-start(f32[16,8,3,4096]{3,1,2,0:T(8,128)} %copy_select_fusion), calls=%async_computation.1 | async-start | bytes 12582912 | tf_op jit(solution)/shard_map/all_to_all | solution.py:40
  82.0 150.4 %reduce-scatter.2.cloned.1.call-start = ((), (), s32[]{:S(2)}) async-start(), calls=%async_computation.4 | async-start | bytes 1572864 | tf_op jit(solution)/shard_map/reduce_scatter | solution.py:47
  85.9 179.4 %all-gather.2.cloned.1.call-start = ((), (), s32[]{:S(2)}) async-start(), calls=%async_computation.5 | async-start | bytes 1572864 | tf_op jit(solution)/shard_map/all_gather | solution.py:61
  232.4 35.2 %copy-start.1 = (f32[1,64,8192]{2,1,0:T(8,128)S(1)}, f32[1,64,8192]{2,1,0:T(8,128)}, u32[]{:S(2)}) copy-start(f32[1,64,8192]{2,1,0:T(8,128)} %param.8) | copy-start | bytes 6291460
Sparse Core Ops, SparseCore 0:
  86.1 11.4 reduce-scatter.1
  239.0 26.2 all-gather.1
where the time goes:
time: 276 us; the launch traced here: 274 us
  waiting for transfers between devices  152 us (55%)
  local copies, waits for them, and re-layouts  42.3 us (15%)
  other arithmetic  38.7 us (14%)
  starting transfers between devices  22.2 us (8%)
  between operations  14.2 us (5%)
  blocking collectives  5.16 us (2%)
    all_to_all x1, waiting for transfers between devices, shards(): lax.all_to_all(send_states, 'fsdp', split_axis=0, concat_axis=0, tiled=True)  120 us
    all_gather x1, waiting for transfers between devices, shards(): lax.all_gather(new_master.astype(jnp.bfloat16), 'replica', axis=1, tiled=...  21.2 us
    select_n x2, other arithmetic, shards(): jnp.take(states, source_row, axis=0).reshape(peers, capacity, 3, width)  11.6 us
    gather x1, local copies, waits for them, and re-layouts, shards(): jnp.take(states, source_row, axis=0).reshape(peers, capacity, 3, width)  11.5 us
    all_to_all x1, waiting for transfers between devices, shards(): lax.all_to_all(send_grads, 'fsdp', split_axis=0, concat_axis=0, tiled=True)  11 us
    all_to_all x1, local copies, waits for them, and re-layouts, shards(): lax.all_to_all(send_states, 'fsdp', split_axis=0, concat_axis=0, tiled=True)  10.4 us
    all_to_all x1, starting transfers between devices, shards(): lax.all_to_all(send_states, 'fsdp', split_axis=0, concat_axis=0, tiled=True)  8.83 us
    gather x1, local copies, waits for them, and re-layouts, shards(): jnp.take(got_states.reshape(peers * capacity, 3, width), order, axis=0)  8.14 us
  transfers between devices with their start and end apart: 5, of which 3 were waited for; matrix products, arithmetic and copies ran while one was open for 25% of the time, Pallas kernels for 0%

commit v1 on v0

v1 whole, which is shorter than its diff:
```python
import functools
import math

import jax
import jax.numpy as jnp
from jax import lax
from jax.experimental import pallas as pl
from jax.experimental.pallas import tpu as pltpu
from jax.sharding import PartitionSpec as P

LANES = 128
TILE_ROWS = 16
VMEM_BYTES = 40 * 1024 * 1024
F32 = jnp.float32
BF16 = jnp.bfloat16


def iota(shape, axis):
    return lax.broadcasted_iota(jnp.int32, shape, axis)


def prepare_kernel(rows, cap, lines, scale, rep_ref, new_row_ref, master_ref, pick_ref, meta_ref):
    width = master_ref.shape[1]
    slots, stacked = pick_ref.shape
    column = iota((1, width), 1) + rep_ref[0] * width
    weights = 1.0 + (column % 7).astype(F32) / 7.0
    part = jnp.sum(master_ref[...] * weights, axis=1, keepdims=True) * scale
    line = new_row_ref[...]
    target = line // rows
    at_row, at_lane = iota((rows, stacked), 0), iota((rows, stacked), 1)
    diagonal = at_row == at_lane
    as_column = jnp.sum(jnp.where(diagonal, line.astype(F32), 0.0), axis=1, keepdims=True).astype(jnp.int32)
    target_column = as_column // rows
    earlier = (target_column == target) & (at_row < at_lane % rows)
    rank = jnp.sum(jnp.where(earlier, 1.0, 0.0), axis=0, keepdims=True).astype(jnp.int32)
    slot = target * lines + (iota((1, stacked), 1) // rows) * cap + rank
    pick = jnp.where(iota((slots, stacked), 0) == slot, 1.0, 0.0).astype(BF16)
    pick_ref[...] = pick
    offset = (as_column - target_column * rows + 1).astype(F32)
    high = part.astype(BF16).astype(F32)
    middle = (part - high).astype(BF16).astype(F32)
    low = part - high - middle
    lane = iota((rows, LANES), 1)
    meta = jnp.where(
        lane == 0, offset, jnp.where(lane == 1, high, jnp.where(lane == 2, middle, jnp.where(lane == 3, low, 0.0)))
    ).astype(BF16)
    meta = jnp.concatenate([meta] * (stacked // rows), axis=0)
    meta_ref[...] = jnp.dot(pick, meta, preferred_element_type=F32).astype(BF16)


def update_kernel(split, cb, body_cols, rep_ref, pick_ref, meta_ref, master_ref, one_ref, two_ref, own_ref, *rest):
    received, (master_out, moments_out) = rest[:-2], rest[-2:]
    j = pl.program_id(0)
    pieces = ([], [], [])
    for h in range(split):
        cols = slice(h * cb, (h + 1) * cb)
        summed = own_ref[:, cols]
        for other in received:
            summed = summed + other[:, cols].astype(F32)
        moved = master_ref[:, cols]
        new_one = 0.9 * one_ref[:, cols] + 0.1 * summed
        new_two = 0.95 * two_ref[:, cols] + 0.05 * summed * summed
        update = new_one / (1.0 - 0.9**10) / (jnp.sqrt(new_two / (1.0 - 0.95**10)) + 1e-08)
        new_master = moved - 0.05 * (update + 0.1 * moved)
        for piece, value in zip(pieces, (new_master, new_one, new_two)):
            piece.append(value.astype(BF16))
    pick = pick_ref[...]
    packed = [jnp.dot(pick, jnp.concatenate(piece, axis=0), preferred_element_type=F32).astype(BF16) for piece in pieces]
    master_out[:, pl.ds(pl.multiple_of(j * cb, LANES), cb)] = packed[0]
    moments_out[:, :cb] = packed[1]
    moments_out[:, cb:] = packed[2]

    @pl.when(j == 0)
    def _():
        master_out[:, body_cols:] = meta_ref[...]


def placing(meta, rows, cap, lines, stacked):
    shape = (meta.shape[0], stacked)
    offset = meta[:, :1].astype(F32).astype(jnp.int32)
    piece = (iota((meta.shape[0], 1), 0) % lines) // cap
    wanted = jnp.where(offset > 0, offset - 1 + piece * rows, -1)
    return jnp.where(iota(shape, 1) == wanted, 1.0, 0.0).astype(BF16)


def placed(place, values):
    return lax.dot_general(place, values, (((0,), (0,)), ((), ())), preferred_element_type=F32)


def master_kernel(rows, cap, lines, cb, blocks, rep_ref, *refs):
    received, (new_master, params, checksum) = refs[:-3], refs[-3:]
    copies = len(received)
    split = lines // cap
    body_cols = blocks * cb
    width = split * body_cols
    place = placing(received[0][:, body_cols:], rows, cap, lines, split * rows)
    total = jnp.zeros((1, rows), F32)
    for k, ref in enumerate(received):
        replica = lax.rem(rep_ref[0] + copies - k, copies)
        base = pl.multiple_of(replica * width, LANES)
        for j in range(blocks):
            rows_out = placed(place, ref[:, j * cb : (j + 1) * cb])
            for h in range(split):
                values = rows_out[h * rows : (h + 1) * rows]
                at = (j * split + h) * cb
                if k == 0:
                    new_master[:, at : at + cb] = values
                params[:, pl.ds(base + at, cb)] = values.astype(BF16)
        sums = placed(ref[:, body_cols:], place)
        total = total + (sums[1:2, :rows] + sums[2:3, :rows] + sums[3:4, :rows])
    checksum[...] = total


def moments_kernel(rows, cap, lines, cb, meta_ref, moments_ref, one_out, two_out):
    split = lines // cap
    place = placing(meta_ref[...], rows, cap, lines, split * rows)
    for at, out in ((0, one_out), (cb, two_out)):
        rows_out = placed(place, moments_ref[:, at : at + cb])
        for h in range(split):
            out[:, h * cb : (h + 1) * cb] = rows_out[h * rows : (h + 1) * rows]


def whole(shape):
    return pl.BlockSpec(shape, lambda *_: (0,) * len(shape))


def shards(master, moment_one, moment_two, gradients, new_row):
    rows, width = master.shape
    peers = lax.axis_size("fsdp")
    copies = lax.axis_size("replica")
    cap = max(2, 2 * rows // peers)
    split = max(1, TILE_ROWS // cap)
    lines = cap * split
    slots = peers * lines
    stacked = split * rows
    body_cols = width // split
    cb = math.gcd(body_cols, 512)
    blocks = body_cols // cb
    span = split * cb
    params_compiler = pltpu.CompilerParams(vmem_limit_bytes=VMEM_BYTES)
    smem = pl.BlockSpec(memory_space=pltpu.SMEM)
    vmem = pl.BlockSpec(memory_space=pltpu.VMEM)

    replica = lax.axis_index("replica").astype(jnp.int32)
    rep = replica.reshape(1)
    full = gradients[0]
    received = []
    for k in range(1, copies):
        other = lax.rem(replica + k, copies)
        part = lax.dynamic_slice(full, (0, other * width), (rows, width)).astype(BF16)
        received.append(lax.ppermute(part, "replica", [(i, (i + k) % copies) for i in range(copies)]))

    pick, meta = pl.pallas_call(
        functools.partial(prepare_kernel, rows, cap, lines, 1.0 / math.sqrt(width * copies)),
        out_shape=(jax.ShapeDtypeStruct((slots, stacked), BF16), jax.ShapeDtypeStruct((slots, LANES), BF16)),
        in_specs=[smem, vmem, vmem],
        out_specs=(vmem, vmem),
        compiler_params=params_compiler,
        cost_estimate=pl.CostEstimate(flops=4 * rows * width, bytes_accessed=4 * rows * width, transcendentals=0),
        name="prepare",
    )(rep, jnp.tile(new_row, split).reshape(1, stacked), master)

    block = pl.BlockSpec((rows, span), lambda j, rep: (0, j))
    send_master, send_moments = pl.pallas_call(
        functools.partial(update_kernel, split, cb, body_cols),
        out_shape=(
            jax.ShapeDtypeStruct((slots, body_cols + LANES), BF16),
            jax.ShapeDtypeStruct((slots, 2 * body_cols), BF16),
        ),
        grid_spec=pltpu.PrefetchScalarGridSpec(
            num_scalar_prefetch=1,
            grid=(blocks,),
            in_specs=[
                whole((slots, stacked)),
                whole((slots, LANES)),
                block,
                block,
                block,
                pl.BlockSpec((rows, span), lambda j, rep: (0, rep[0] * blocks + j)),
            ]
            + [block] * (copies - 1),
            out_specs=(
                whole((slots, body_cols + LANES)),
                pl.BlockSpec((slots, 2 * cb), lambda j, rep: (0, j)),
            ),
        ),
        compiler_params=params_compiler,
        cost_estimate=pl.CostEstimate(
            flops=6 * slots * stacked * body_cols, bytes_accessed=24 * rows * width, transcendentals=rows * width
        ),
        name="update",
    )(rep, pick, meta, master, moment_one, moment_two, full, *received)

    got_master = lax.all_to_all(send_master, "fsdp", split_axis=0, concat_axis=0, tiled=True)
    got_moments = lax.all_to_all(send_moments, "fsdp", split_axis=0, concat_axis=0, tiled=True)

    got = [got_master] + [
        lax.ppermute(got_master, "replica", [(i, (i + k) % copies) for i in range(copies)]) for k in range(1, copies)
    ]
    new_master, params, checksum = pl.pallas_call(
        functools.partial(master_kernel, rows, cap, lines, cb, blocks),
        out_shape=(
            jax.ShapeDtypeStruct((rows, width), F32),
            jax.ShapeDtypeStruct((rows, width * copies), BF16),
            jax.ShapeDtypeStruct((1, rows), F32),
        ),
        in_specs=[smem] + [vmem] * copies,
        out_specs=(vmem, vmem, vmem),
        compiler_params=params_compiler,
        cost_estimate=pl.CostEstimate(
            flops=2 * copies * slots * stacked * body_cols, bytes_accessed=12 * rows * width, transcendentals=0
        ),
        name="place_master",
    )(rep, *got)

    new_one, new_two = pl.pallas_call(
        functools.partial(moments_kernel, rows, cap, lines, cb),
        out_shape=(jax.ShapeDtypeStruct((rows, width), F32), jax.ShapeDtypeStruct((rows, width), F32)),
        grid=(blocks,),
        in_specs=[
            pl.BlockSpec((slots, LANES), lambda j: (0, body_cols // LANES)),
            pl.BlockSpec((slots, 2 * cb), lambda j: (0, j)),
        ],
        out_specs=(pl.BlockSpec((rows, span), lambda j: (0, j)), pl.BlockSpec((rows, span), lambda j: (0, j))),
        compiler_params=params_compiler,
        cost_estimate=pl.CostEstimate(
            flops=4 * slots * stacked * body_cols, bytes_accessed=16 * rows * width, transcendentals=0
        ),
        name="place_moments",
    )(got_master, got_moments)
    return (new_master, new_one, new_two, params, checksum.reshape(rows))


def solution(mesh):
    return jax.shard_map(
        shards,
        mesh=mesh,
        in_specs=(
            P("fsdp", "replica"),
            P("fsdp", "replica"),
            P("fsdp", "replica"),
            P("replica", "fsdp", None),
            P("fsdp"),
        ),
        out_specs=(
            P("fsdp", "replica"),
            P("fsdp", "replica"),
            P("fsdp", "replica"),
            P("fsdp", None),
            P("fsdp"),
        ),
        check_vma=False,
    )
```

time: 276 us -> 103 us (0.37)
  the two profiles are of different devices: /device:TPU:5 before, /device:TPU:12 now
where the time goes in v1:
time: 103 us; the launch traced here: 102 us
  waiting for transfers between devices  46.1 us (45%)
  blocking collectives  34.2 us (33%)
  Pallas kernels  8 us (8%)
  local copies, waits for them, and re-layouts  7.38 us (7%)
  starting transfers between devices  5.84 us (6%)
    all_to_all x1, waiting for transfers between devices, shards(): lax.all_to_all(send_moments, 'fsdp', split_axis=0, concat_axis=0, tiled=T...  43.3 us
    all_to_all x1, blocking collectives, shards(): lax.all_to_all(send_master, 'fsdp', split_axis=0, concat_axis=0, tiled=True)  34.2 us
    all_to_all x1, starting transfers between devices, shards(): lax.all_to_all(send_moments, 'fsdp', split_axis=0, concat_axis=0, tiled=T...  5.77 us
    unnamed x12, local copies, waits for them, and re-layouts  5.27 us
    pallas_call x1, Pallas kernels, shards(): pl.pallas_call(functools.partial(update_kernel, split, cb, body_cols), ou...  2.96 us
    pallas_call x1, Pallas kernels, shards(): pl.pallas_call(functools.partial(moments_kernel, rows, cap, lines, cb), o...  2.75 us
    ppermute x1, waiting for transfers between devices, shards(): lax.ppermute(got_master, 'replica', [(i, (i + k) % copies) for i in range...  2.75 us
  transfers between devices with their start and end apart: 3, of which 2 were waited for; matrix products, arithmetic and copies ran while one was open for 1% of the time, Pallas kernels for 2%

profile of v1, /device:TPU:12, one launch (start us, length us, event | category | flops | bytes accessed | tf_op | source)
XLA Modules:
  0.0 102.2 jit_solution(10285272384685855234)
XLA Ops:
  0.6 0.0 copy-start.1
  0.7 1.4 %fusion = bf16[64,4096]{1,0:T(8,128)(2,1)S(1)} fusion(f32[1,64,8192]{2,1,0:T(8,128)} %param.8, s32[]{:T(128)S(6)} %select_n.3), kind=kLoop, calls=%fused_computation.1 | loop fusion | bytes 1048580 | tf_op jit(solution)/shard_map/convert_element_type | solution.py:150
  2.0 0.1 collective-permute-start
  2.1 0.7 tile.2
  2.8 0.1 reshape_tile.3.new_row_ref
  2.8 0.0 copy-start
  2.8 1.2 %copy-done = f32[64,4096]{1,0:T(8,128)S(1)} copy-done((f32[64,4096]{1,0:T(8,128)S(1)}, f32[64,4096]{1,0:T(8,128)}, u32[]{:S(2)}) %copy-start) | copy-done | bytes 1048600
  4.1 0.5 prepare.1
  4.5 0.0 collective-permute-done.rest_0_
  4.5 0.0 copy-done.1
  4.5 0.0 copy-start.2
  4.6 1.6 %copy-done.2 = f32[1,64,8192]{2,1,0:T(8,128)S(1)} copy-done((f32[1,64,8192]{2,1,0:T(8,128)S(1)}, f32[1,64,8192]{2,1,0:T(8,128)}, u32[]{:S(2)}) %copy-start.2) | copy-done | bytes 2097176
  6.1 1.2 %copy-done.4 = f32[64,4096]{1,0:T(8,128)S(1)} copy-done((f32[64,4096]{1,0:T(8,128)S(1)}, f32[64,4096]{1,0:T(8,128)}, u32[]{:S(2)}) %copy-start.4) | copy-done | bytes 1048600
  7.4 1.2 %copy-done.5 = f32[64,4096]{1,0:T(8,128)S(1)} copy-done((f32[64,4096]{1,0:T(8,128)S(1)}, f32[64,4096]{1,0:T(8,128)}, u32[]{:S(2)}) %copy-start.5) | copy-done | bytes 1048600
  8.6 3.0 %update.1 = (bf16[256,2176]{1,0:T(8,128)(2,1)S(1)}, bf16[256,4096]{1,0:T(8,128)(2,1)S(1)}) custom-call(s32[1]{0:T(128)} %bitcast.rep_ref, bf16[256,128]{1,0:T(8,128)(2,1)S(1)} %get-tuple-element.14.pick_ref, bf16[256,128]{1,0:T(8,128)(2,1)S(1)} %get-tuple-element.15.meta_ref, f32[64,4096]{1,0:T(8,128)S(1)} %copy-done.1, f32[64,4096]{1,0:T(8,128)S(1)} %copy-done.4, ...), custom_call_target="tpu_custom_call" | custom-call | flops 402653184 | bytes 6291456 | tf_op jit(solution)/shard_map/update/pallas_call | solution.py:164
  11.6 0.0 copy-start.3
  11.6 34.2 %all_to_all.22 = bf16[16,16,2176]{2,1,0:T(8,128)(2,1)S(1)} all-to-all(bf16[16,16,2176]{2,1,0:T(8,128)(2,1)S(1)} %bitcast.15), channel_id=1, replica_groups=mesh['fsdp'=16,'replica'=2] {'fsdp'}, dimensions={0} | all-to-all | bytes 2228224 | tf_op jit(solution)/shard_map/all_to_all | solution.py:194
  45.8 0.0 copy-done.3
  45.8 5.8 %all-to-all-start.1 = ((bf16[16,16,4096]{2,1,0:T(8,128)(2,1)}), bf16[16,16,4096]{2,1,0:T(8,128)(2,1)S(1)}, u32[]{:S(2)}, u32[]{:S(2)}) async-start(bf16[16,16,4096]{2,1,0:T(8,128)(2,1)} %bitcast.14), calls=%async_computation.1 | async-start | bytes 4194304 | tf_op jit(solution)/shard_map/all_to_all | solution.py:195
  51.5 0.0 collective-permute-start.1
  51.5 2.7 %collective-permute-done.1.refs_1_ = bf16[256,2176]{1,0:T(8,128)(2,1)S(1)} collective-permute-done((bf16[256,2176]{1,0:T(8,128)(2,1)S(1)}, bf16[256,2176]{1,0:T(8,128)(2,1)S(1)}, u32[]{:S(2)}, u32[]{:S(2)}) %collective-permute-start.1) | collective-permute-done | bytes 1114144 | tf_op jit(solution)/shard_map/ppermute | solution.py:198
  54.3 1.8 %place_master.1 = (f32[64,4096]{1,0:T(8,128)}, bf16[64,8192]{1,0:T(8,128)(2,1)}, f32[1,64]{1,0:T(1,128)}) custom-call(s32[1]{0:T(128)} %bitcast.rep_ref, bf16[256,2176]{1,0:T(8,128)(2,1)S(1)} %bitcast.10, bf16[256,2176]{1,0:T(8,128)(2,1)S(1)} %collective-permute-done.1.refs_1_), custom_call_target="tpu_custom_call" | custom-call | flops 268435456 | bytes 3145728 | tf_op jit(solution)/shard_map/place_master/pallas_call | solution.py:200
  56.1 43.3 %all-to-all-done.1 = bf16[16,16,4096]{2,1,0:T(8,128)(2,1)S(1)} async-done(((bf16[16,16,4096]{2,1,0:T(8,128)(2,1)}), bf16[16,16,4096]{2,1,0:T(8,128)(2,1)S(1)}, u32[]{:S(2)}, u32[]{:S(2)}) %all-to-all-start.1) | async-done | bytes 2097184 | tf_op jit(solution)/shard_map/all_to_all | solution.py:195
  99.4 2.8 %place_moments.1 = (f32[64,4096]{1,0:T(8,128)}, f32[64,4096]{1,0:T(8,128)}) custom-call(bf16[256,2176]{1,0:T(8,128)(2,1)S(1)} %bitcast.11, bf16[256,4096]{1,0:T(8,128)(2,1)S(1)} %bitcast.12), custom_call_target="tpu_custom_call" | custom-call | flops 268435456 | bytes 4194304 | tf_op jit(solution)/shard_map/place_moments/pallas_call | solution.py:216
  (2 shorter events, 0.0 us)
Async XLA Ops:
  0.6 3.9 %copy-start.1 = (f32[64,4096]{1,0:T(8,128)S(1)}, f32[64,4096]{1,0:T(8,128)}, u32[]{:S(2)}) copy-start(f32[64,4096]{1,0:T(8,128)} %master_ref.3) | copy-start | bytes 3145732
  2.0 2.5 %collective-permute-start = (bf16[64,4096]{1,0:T(8,128)(2,1)S(1)}, bf16[64,4096]{1,0:T(8,128)(2,1)S(1)}, u32[]{:S(2)}, u32[]{:S(2)}) collective-permute-start(bf16[64,4096]{1,0:T(8,128)(2,1)S(1)} %fusion), channel_id=1, source_target_pairs={{0,1},{1,0},{2,3},{3,2},{4,5},{5,4},{6,7},{7,6},{8,9},{9,8},{10,11... | collective-permute-start | bytes 1572872 | tf_op jit(solution)/shard_map/ppermute | solution.py:151
  2.8 1.2 %copy-start = (f32[64,4096]{1,0:T(8,128)S(1)}, f32[64,4096]{1,0:T(8,128)}, u32[]{:S(2)}) copy-start(f32[64,4096]{1,0:T(8,128)} %master_ref.3) | copy-start | bytes 3145732
  4.5 1.6 %copy-start.2 = (f32[1,64,8192]{2,1,0:T(8,128)S(1)}, f32[1,64,8192]{2,1,0:T(8,128)}, u32[]{:S(2)}) copy-start(f32[1,64,8192]{2,1,0:T(8,128)} %param.8) | copy-start | bytes 6291460
  6.1 1.2 %copy-start.4 = (f32[64,4096]{1,0:T(8,128)S(1)}, f32[64,4096]{1,0:T(8,128)}, u32[]{:S(2)}) copy-start(f32[64,4096]{1,0:T(8,128)} %one_ref.1) | copy-start | bytes 3145732
  7.4 1.2 %copy-start.5 = (f32[64,4096]{1,0:T(8,128)S(1)}, f32[64,4096]{1,0:T(8,128)}, u32[]{:S(2)}) copy-start(f32[64,4096]{1,0:T(8,128)} %two_ref.1) | copy-start | bytes 3145732
  11.6 34.2 %copy-start.3 = (bf16[256,4096]{1,0:T(8,128)(2,1)}, bf16[256,4096]{1,0:T(8,128)(2,1)S(1)}, u32[]{:S(2)}) copy-start(bf16[256,4096]{1,0:T(8,128)(2,1)S(1)} %get-tuple-element.18) | copy-start | bytes 6291460
  45.8 53.7 %all-to-all-start.1 = ((bf16[16,16,4096]{2,1,0:T(8,128)(2,1)}), bf16[16,16,4096]{2,1,0:T(8,128)(2,1)S(1)}, u32[]{:S(2)}, u32[]{:S(2)}) async-start(bf16[16,16,4096]{2,1,0:T(8,128)(2,1)} %bitcast.14), calls=%async_computation.1 | async-start | bytes 4194304 | tf_op jit(solution)/shard_map/all_to_all | solution.py:195
  51.5 2.8 %collective-permute-start.1 = (bf16[256,2176]{1,0:T(8,128)(2,1)S(1)}, bf16[256,2176]{1,0:T(8,128)(2,1)S(1)}, u32[]{:S(2)}, u32[]{:S(2)}) collective-permute-start(bf16[256,2176]{1,0:T(8,128)(2,1)S(1)} %bitcast.9), channel_id=1, source_target_pairs={{0,1},{1,0},{2,3},{3,2},{4,5},{5,4},{6,7},{7,6},{8,9},{9,8},{10,11... | collective-permute-start | bytes 3342344 | tf_op jit(solution)/shard_map/ppermute | solution.py:198
